TPU v7x, 256 devices: a whole 4x4x8 slice. The times are simulated.
256 devices in a mesh: depth: 64 (over x_hi, y, z), band: 4 (over x_lo, core).
Axes of the slice: x: 4 (x_hi: 2, x_lo: 2; x = x_hi * 2 + x_lo), y: 4, z: 8, core: 2. Of those that a mesh axis runs over, the one named last changes fastest.
Arguments:
- planes: float32 [64, 256, 2048], P('depth', 'band'), may hold values from -6 to 6
- denoised: float32 [64, 256, 2048], P('depth', 'band'), may hold values from -6 to 6
- scaled_dual: float32 [64, 256, 2048], P('depth', 'band'), may hold values from -4 to 4
- measured: float32 [256, 2048], P('band'), may hold values from -6 to 6
- lenslet_psf: bfloat16 [64, 31, 31], P('depth'), may hold values from -0.0234375 to 0.0234375
- kernel: bfloat16 [27, 16], replicated, may hold values from -1.25 to 1.25
- layer_bias: float32 [16], replicated, may hold values from -3 to 3
- mix_weight: bfloat16 [16], replicated, may hold values from -1.5 to 1.5
Outputs:
- new_planes: float32 [64, 256, 2048], P('depth', 'band')
- new_denoised: float32 [64, 256, 2048], P('depth', 'band')
- new_dual: float32 [64, 256, 2048], P('depth', 'band')
All inputs are finite; a program needn't handle non-finite values.
Results may differ from a plain program's by a relative error of at most 0.0049.
Values may be sent and summed in bfloat16 or wider, within the bound.
No kernel may reach another device: no remote copies, remote signals or barrier semaphores. Data moves between devices by JAX's collectives and lax.ppermute only.
A program may use at most 128 MiB of HBM per device.

v0:
```python
import jax
import jax.numpy as jnp
from jax import lax
from jax.sharding import PartitionSpec as P

KS = 31
step_size = 4.0
penalty = 0.5


def padded_2(block, sides, width):
    for axis, dim in sides:
        count = lax.axis_size(axis)
        forward = [(i, i + 1) for i in range(count - 1)]
        backward = [(target, source) for source, target in forward]
        low = lax.ppermute(
            lax.slice_in_dim(block, block.shape[dim] - width, None, axis=dim), axis, forward
        )
        high = lax.ppermute(lax.slice_in_dim(block, 0, width, axis=dim), axis, backward)
        block = jnp.concatenate([low, block, high], axis=dim)
    return block


def project(rimmed, psf_one):
    span_rows = rimmed.shape[0] - KS + 1
    total_cols = rimmed.shape[1]
    col_block = 256
    window_cols = col_block + KS - 1
    edge = KS // 2
    padded = jnp.pad(rimmed, ((0, 0), (edge, edge)))
    offsets = jnp.arange(window_cols)[:, None] - jnp.arange(col_block)[None, :]
    onehot = (offsets[None] == jnp.arange(KS)[:, None, None]).astype(jnp.bfloat16)
    band_matrix = jnp.einsum("ab,btj->atj", psf_one, onehot, preferred_element_type=jnp.float32)
    band_matrix = band_matrix.astype(jnp.bfloat16).reshape(KS * window_cols, col_block)
    pieces = []
    for b in range(total_cols // col_block):
        window = padded[:, b * col_block : b * col_block + window_cols]
        stacked = jnp.stack([window[a : a + span_rows] for a in range(KS)], axis=1)
        stacked = stacked.reshape(span_rows, KS * window_cols)
        pieces.append(jnp.dot(stacked, band_matrix, preferred_element_type=jnp.float32))
    return jnp.concatenate(pieces, axis=1)


def shards(planes, denoised, scaled_dual, measured, lenslet_psf, kernel, layer_bias, mix_weight):
    plane_count, band_rows, total_cols = planes.shape
    edge = KS // 2
    planes_half = planes.astype(jnp.bfloat16)
    rimmed = padded_2(planes_half, (("band", 1),), edge)
    partial_value = project(rimmed[0], lenslet_psf[0])
    sensor = lax.psum(partial_value, "depth")
    residual = (sensor - measured).astype(jnp.bfloat16)
    residual_rimmed = padded_2(residual, (("band", 0),), edge)
    gradient = jnp.stack([project(residual_rimmed, lenslet_psf[0][::-1, ::-1])])
    new_planes = planes - step_size * (gradient + penalty * (planes - (denoised - scaled_dual)))
    noisy = new_planes + scaled_dual
    noisy_half = noisy.astype(jnp.bfloat16)
    volume = padded_2(noisy_half, (("depth", 0), ("band", 1)), 1)
    volume = jnp.pad(volume, ((0, 0), (0, 0), (1, 1)))
    taps = []
    for i in range(3):
        for j in range(3):
            for k in range(3):
                taps.append(volume[i : i + plane_count, j : j + band_rows, k : k + total_cols])
    stacked = jnp.stack(taps)
    hidden = jnp.einsum("kn,kprc->nprc", kernel, stacked, preferred_element_type=jnp.float32)
    hidden = jnp.maximum(hidden + layer_bias[:, None, None, None], 0.0).astype(jnp.bfloat16)
    noise = jnp.einsum("n,nprc->prc", mix_weight, hidden, preferred_element_type=jnp.float32)
    new_denoised = noisy - noise
    new_dual = scaled_dual + new_planes - new_denoised
    return (new_planes, new_denoised, new_dual)


def solution(mesh):
    in_specs = (
        P("depth", "band", None),
        P("depth", "band", None),
        P("depth", "band", None),
        P("band", None),
        P("depth", None, None),
        P(),
        P(),
        P(),
    )
    out_specs = (P("depth", "band", None), P("depth", "band", None), P("depth", "band", None))
    return jax.shard_map(shards, mesh=mesh, in_specs=in_specs, out_specs=out_specs, check_vma=False)
```

profile of v0, /device:TPU:5, one launch (start us, length us, event | category | flops | bytes accessed | tf_op | source)
XLA Modules:
  0.0 905.9 jit_solution(1731038789126102001)
XLA Ops:
  7.2 1.1 convert_element_type.35
  8.3 3.4 collective-permute-start
  11.7 1.9 collective-permute-start.1
  13.7 2.9 convert_bitcast_fusion.1
  18.2 1.2 constant_dynamic-update-slice_fusion.153
  19.3 1.2 constant_dynamic-update-slice_fusion.152
  20.5 1.2 constant_dynamic-update-slice_fusion.151
  21.6 1.2 constant_dynamic-update-slice_fusion.150
  22.8 1.2 constant_dynamic-update-slice_fusion.149
  24.0 1.2 constant_dynamic-update-slice_fusion.148
  25.1 1.2 constant_dynamic-update-slice_fusion.147
  26.3 1.1 constant_dynamic-update-slice_fusion.146
  27.4 1.2 constant_dynamic-update-slice_fusion.145
  28.6 1.2 constant_dynamic-update-slice_fusion.144
  29.7 1.2 constant_dynamic-update-slice_fusion.143
  30.9 1.2 constant_dynamic-update-slice_fusion.142
  32.1 1.2 constant_dynamic-update-slice_fusion.141
  33.2 1.2 constant_dynamic-update-slice_fusion.140
  34.4 1.2 constant_dynamic-update-slice_fusion.139
  35.6 1.1 constant_dynamic-update-slice_fusion.138
  36.6 1.2 constant_dynamic-update-slice_fusion.137
  37.8 1.2 constant_dynamic-update-slice_fusion.136
  39.0 1.2 constant_dynamic-update-slice_fusion.135
  40.2 1.2 constant_dynamic-update-slice_fusion.134
  41.4 1.2 constant_dynamic-update-slice_fusion.133
  42.5 1.2 constant_dynamic-update-slice_fusion.132
  43.7 1.2 constant_dynamic-update-slice_fusion.131
  44.9 1.1 constant_dynamic-update-slice_fusion.130
  45.9 1.2 constant_dynamic-update-slice_fusion.129
  47.1 1.2 constant_dynamic-update-slice_fusion.128
  55.7 5.2 fusion.30
  61.0 5.1 fusion.29
  66.0 5.3 fusion.28
  71.3 5.1 fusion.27
  76.3 5.5 fusion.26
  81.9 5.1 fusion.25
  86.9 5.1 fusion.24
  92.0 5.7 fusion.23
  97.7 0.8 copy-done.5
  98.6 645.6 %all-reduce.5.cloned.1.call-done = f32[64,2048]{1,0:T(8,128)} async-done(((f32[64,2048]{1,0:T(8,128)}), f32[64,2048]{1,0:T(8,128)}) %all-reduce.5.cloned.1.call-update) | async-done | bytes 524304 | tf_op jit(solution)/shard_map/psum | solution.py:50
  744.2 1.1 subtract_convert_fusion
  745.4 49.2 %collective-permute-start.2 = (bf16[15,2048]{1,0:T(8,128)(2,1)S(1)}, bf16[15,2048]{1,0:T(8,128)(2,1)S(1)}, u32[]{:S(2)}, u32[]{:S(2)}) collective-permute-start(bf16[15,2048]{1,0:T(8,128)(2,1)S(1)} %get-tuple-element.349), channel_id=1, source_target_pairs={{0,1},{1,2},{2,3},{4,5},{5,6},{6,7},{8,9},{9,10},{10,11},{12,13},{... | collective-permute-start | bytes 184328 | tf_op jit(solution)/shard_map/ppermute | solution.py:16
  794.6 2.2 convert_bitcast_fusion
  796.8 1.9 collective-permute-start.3
  800.5 1.9 collective-permute-done.3
  812.7 5.5 fusion.22
  823.6 5.0 fusion.21
  828.6 5.2 fusion.20
  833.8 5.1 fusion.19
  838.9 5.1 fusion.18
  844.0 5.5 fusion.17
  849.4 5.1 fusion.16
  854.5 5.2 fusion.15
  859.8 1.0 fusion.249
  860.7 2.3 collective-permute-start.4
  863.0 8.7 collective-permute-start.5
  871.7 2.8 collective-permute-done.4
  874.5 1.6 collective-permute-done.5
  876.2 2.1 collective-permute-start.6
  878.3 2.2 collective-permute-start.7
  880.6 2.9 collective-permute-done.7
  886.6 2.9 copy-done.9
  889.6 8.1 fusion.8
  897.6 1.2 fusion.248
  (304 shorter events, 29.1 us)
Async XLA Ops:
  7.2 882.4 %copy-start = (bf16[27,16]{0,1:T(8,128)(2,1)S(1)}, bf16[27,16]{0,1:T(8,128)(2,1)}, u32[]{:S(2)}) copy-start(bf16[27,16]{0,1:T(8,128)(2,1)} %param.13) | copy-start | bytes 2596
  7.2 737.0 %all-reduce.5.cloned.1.call-start = ((), (), s32[]{:S(2)}) async-start(), calls=%async_computation | async-start | bytes 1048576 | tf_op jit(solution)/shard_map/psum | solution.py:50
  8.3 8.3 collective-permute-start
  11.7 5.6 collective-permute-start.1
  17.4 0.7 copy-start.1
  39.0 9.3 %copy-start.2 = (bf16[94,2048]{1,0:T(8,128)(2,1)S(1)}, bf16[94,2048]{1,0:T(8,128)(2,1)}, u32[]{:S(2)}) copy-start(bf16[94,2048]{1,0:T(8,128)(2,1)} %copy-done.1) | copy-start | bytes 1155076
  92.0 6.5 copy-start.8
  92.0 652.2 %copy-start.4 = (f32[64,2048]{1,0:T(8,128)S(1)}, f32[64,2048]{1,0:T(8,128)}, u32[]{:S(2)}) copy-start(f32[64,2048]{1,0:T(8,128)} %param.11) | copy-start | bytes 1572868
  97.7 0.8 copy-start.5
  745.4 53.4 %collective-permute-start.2 = (bf16[15,2048]{1,0:T(8,128)(2,1)S(1)}, bf16[15,2048]{1,0:T(8,128)(2,1)S(1)}, u32[]{:S(2)}, u32[]{:S(2)}) collective-permute-start(bf16[15,2048]{1,0:T(8,128)(2,1)S(1)} %get-tuple-element.349), channel_id=1, source_target_pairs={{0,1},{1,2},{2,3},{4,5},{5,6},{6,7},{8,9},{9,10},{10,11},{12,13},{... | collective-permute-start | bytes 184328 | tf_op jit(solution)/shard_map/ppermute | solution.py:16
  796.8 5.6 collective-permute-start.3
  854.5 5.3 copy-start.3
  854.5 5.3 copy-start.6
  854.5 5.3 copy-start.7
  860.7 13.8 %collective-permute-start.4 = (bf16[1,64,2048]{2,1,0:T(8,128)(2,1)S(1)}, bf16[1,64,2048]{2,1,0:T(8,128)(2,1)S(1)}, u32[]{:S(2)}, u32[]{:S(2)}) collective-permute-start(bf16[1,64,2048]{2,1,0:T(8,128)(2,1)S(1)} %get-tuple-element.5), channel_id=1, source_target_pairs={{0,4},{4,8},{8,12},{12,16},{16,20},{20,24},{24,28},{28,32},{32,36}... | collective-permute-start | bytes 786440 | tf_op jit(solution)/shard_map/ppermute | solution.py:16
  863.0 13.1 %collective-permute-start.5 = (bf16[1,64,2048]{2,1,0:T(8,128)(2,1)S(1)}, bf16[1,64,2048]{2,1,0:T(8,128)(2,1)S(1)}, u32[]{:S(2)}, u32[]{:S(2)}) collective-permute-start(bf16[1,64,2048]{2,1,0:T(8,128)(2,1)S(1)} %get-tuple-element.5), channel_id=1, source_target_pairs={{4,0},{8,4},{12,8},{16,12},{20,16},{24,20},{28,24},{32,28},{36,32}... | collective-permute-start | bytes 786440 | tf_op jit(solution)/shard_map/ppermute | solution.py:19
  876.2 4.3 collective-permute-start.6
  878.3 5.1 collective-permute-start.7
  886.1 3.5 copy-start.10
  886.1 3.4 copy-start.11
  886.6 2.9 copy-start.9
Sparse Core Ops, SparseCore 0:
  98.6 645.5 all-reduce.4
where the time goes:
time: 916 us; the launch traced here: 906 us
  waiting for transfers between devices  656 us (72%)
  matrix products  96.7 us (11%)
  starting transfers between devices  71.8 us (8%)
  local copies, waits for them, and re-layouts  45 us (5%)
  other arithmetic  21.3 us (2%)
  between operations  15.5 us (2%)
    psum x1, waiting for transfers between devices, shards(): sensor = lax.psum(partial_value, 'depth')  646 us
    dot_general x16, matrix products, project(): jnp.dot(stacked, band_matrix, preferred_element_type=jnp.float32)  83.5 us
    ppermute x4, starting transfers between devices, padded_2(): lax.ppermute(lax.slice_in_dim(block, block.shape[dim] - width, None, axis...  57 us
    unnamed x164, local copies, waits for them, and re-layouts  44.4 us
  transfers between devices with their start and end apart: 9, of which 6 were waited for; matrix products, arithmetic and copies ran while one was open for 1% of the time, Pallas kernels for 0%

commit v1 on v0

--- a/solution.py
+++ b/solution.py
@@ -47,7 +47,7 @@
     planes_half = planes.astype(jnp.bfloat16)
     rimmed = padded_2(planes_half, (("band", 1),), edge)
     partial_value = project(rimmed[0], lenslet_psf[0])
-    sensor = lax.psum(partial_value, "depth")
+    sensor = jnp.sum(lax.all_gather(partial_value, "depth"), axis=0)
     residual = (sensor - measured).astype(jnp.bfloat16)
     residual_rimmed = padded_2(residual, (("band", 0),), edge)
     gradient = jnp.stack([project(residual_rimmed, lenslet_psf[0][::-1, ::-1])])

time: 916 us -> 577 us (0.63)
  waiting for transfers between devices: 656 us -> 351 us
  starting transfers between devices: 71.8 us -> 27.3 us
  other arithmetic: 21.3 us -> 31.9 us
    psum x1 -> x0, waiting for transfers between devices: 646 us -> none  [shards(): sensor = lax.psum(partial_value, 'depth')]
    all_gather x0 -> x1, waiting for transfers between devices: none -> 341 us  [shards(): sensor = jnp.sum(lax.all_gather(partial_value, 'depth'), axis=0)]
    ppermute x4, starting transfers between devices: 57 us -> 12.1 us  [padded_2(): lax.ppermute(lax.slice_in_dim(block, block.shape[dim] - width, None, axis...]
    reduce_sum x0 -> x1, other arithmetic: none -> 11.7 us  [shards(): sensor = jnp.sum(lax.all_gather(partial_value, 'depth'), axis=0)]
where the time goes in v1:
time: 577 us; the launch traced here: 567 us
  waiting for transfers between devices  351 us (61%)
  matrix products  96.9 us (17%)
  local copies, waits for them, and re-layouts  45 us (8%)
  other arithmetic  31.9 us (6%)
  starting transfers between devices  27.3 us (5%)
  between operations  15.5 us (3%)
    all_gather x1, waiting for transfers between devices, shards(): sensor = jnp.sum(lax.all_gather(partial_value, 'depth'), axis=0)  341 us
    dot_general x16, matrix products, project(): jnp.dot(stacked, band_matrix, preferred_element_type=jnp.float32)  83.7 us
    unnamed x164, local copies, waits for them, and re-layouts  44.4 us
    ppermute x4, starting transfers between devices, padded_2(): lax.ppermute(lax.slice_in_dim(block, 0, width, axis=dim), axis, backward)  15.2 us
    unnamed x144, other arithmetic  15 us
    ppermute x4, starting transfers between devices, padded_2(): lax.ppermute(lax.slice_in_dim(block, block.shape[dim] - width, None, axis...  12.1 us
    reduce_sum x1, other arithmetic, shards(): sensor = jnp.sum(lax.all_gather(partial_value, 'depth'), axis=0)  11.7 us
  transfers between devices with their start and end apart: 9, of which 6 were waited for; matrix products, arithmetic and copies ran while one was open for 1% of the time, Pallas kernels for 0%

profile of v1, /device:TPU:5, one launch (start us, length us, event | category | flops | bytes accessed | tf_op | source)
XLA Modules:
  0.0 567.1 jit_solution(11259282851413785533)
XLA Ops:
  7.2 1.1 convert_element_type.35
  8.3 3.4 collective-permute-start
  11.7 1.9 collective-permute-start.1
  13.7 2.9 convert_bitcast_fusion.1
  18.2 1.2 constant_dynamic-update-slice_fusion.153
  19.3 1.2 constant_dynamic-update-slice_fusion.152
  20.5 1.2 constant_dynamic-update-slice_fusion.151
  21.6 1.2 constant_dynamic-update-slice_fusion.150
  22.8 1.2 constant_dynamic-update-slice_fusion.149
  24.0 1.2 constant_dynamic-update-slice_fusion.148
  25.1 1.2 constant_dynamic-update-slice_fusion.147
  26.3 1.1 constant_dynamic-update-slice_fusion.146
  27.4 1.2 constant_dynamic-update-slice_fusion.145
  28.6 1.2 constant_dynamic-update-slice_fusion.144
  29.7 1.2 constant_dynamic-update-slice_fusion.143
  30.9 1.2 constant_dynamic-update-slice_fusion.142
  32.1 1.2 constant_dynamic-update-slice_fusion.141
  33.2 1.2 constant_dynamic-update-slice_fusion.140
  34.4 1.2 constant_dynamic-update-slice_fusion.139
  35.6 1.1 constant_dynamic-update-slice_fusion.138
  36.6 1.2 constant_dynamic-update-slice_fusion.137
  37.8 1.2 constant_dynamic-update-slice_fusion.136
  39.0 1.2 constant_dynamic-update-slice_fusion.135
  40.2 1.2 constant_dynamic-update-slice_fusion.134
  41.4 1.2 constant_dynamic-update-slice_fusion.133
  42.5 1.2 constant_dynamic-update-slice_fusion.132
  43.7 1.2 constant_dynamic-update-slice_fusion.131
  44.9 1.1 constant_dynamic-update-slice_fusion.130
  45.9 1.2 constant_dynamic-update-slice_fusion.129
  47.1 1.2 constant_dynamic-update-slice_fusion.128
  55.7 5.2 fusion.30
  61.0 5.1 fusion.29
  66.0 5.3 fusion.28
  71.3 5.1 fusion.27
  76.3 5.5 fusion.26
  81.9 5.1 fusion.25
  86.9 5.1 fusion.24
  92.0 5.9 %fusion.23 = f32[64,2048]{1,0:T(8,128)S(1)} fusion(f32[64,2048]{1,0:T(8,128)S(1)} %fusion.24, bf16[64,31,286]{2,0,1:T(8,128)(2,1)S(1)} %get-tuple-element.72, bf16[31,286,256]{2,0,1:T(8,128)(2,1)S(1)} %convert_bitcast_fusion.1), kind=kOutput, calls=%fused_computation.212 | convolution fusion | flops 290521088 | bytes 6275072 | tf_op jit(solution)/shard_map/dot_general | solution.py:40
  97.8 0.8 copy-done.5
  98.8 340.6 %all-gather.3.cloned.1.call-done = f32[4096,2048]{1,0:T(8,128)} async-done(((f32[64,2048]{1,0:T(8,128)}), f32[4096,2048]{1,0:T(8,128)}) %all-gather.3.cloned.1.call-update) | async-done | bytes 33554448 | tf_op jit(solution)/shard_map/all_gather | solution.py:50
  439.4 11.7 %reduce_sum.9 = f32[64,2048]{1,0:T(8,128)S(1)} reduce(f32[64,64,2048]{2,1,0:T(8,128)} %bitcast.1719, f32[]{:T(128)} %constant.1.clone.1), dimensions={0}, to_apply=%region_0.1 | reduce | flops 8257536 | bytes 34078724 | tf_op jit(solution)/shard_map/reduce_sum | solution.py:50
  451.2 4.7 collective-permute-start.2
  455.8 2.2 convert_bitcast_fusion
  458.1 1.9 collective-permute-start.3
  461.8 1.9 collective-permute-done.3
  474.0 5.5 fusion.22
  484.8 5.0 fusion.21
  489.9 5.2 fusion.20
  495.1 5.1 fusion.19
  500.2 5.1 fusion.18
  505.2 5.5 fusion.17
  510.7 5.1 fusion.16
  515.8 5.2 fusion.15
  521.0 1.0 fusion.249
  522.0 1.9 collective-permute-start.4
  523.9 9.1 %collective-permute-start.5 = (bf16[1,64,2048]{2,1,0:T(8,128)(2,1)S(1)}, bf16[1,64,2048]{2,1,0:T(8,128)(2,1)S(1)}, u32[]{:S(2)}, u32[]{:S(2)}) collective-permute-start(bf16[1,64,2048]{2,1,0:T(8,128)(2,1)S(1)} %get-tuple-element.5), channel_id=1, source_target_pairs={{4,0},{8,4},{12,8},{16,12},{20,16},{24,20},{28,24},{32,28},{36,32}... | collective-permute-start | bytes 786440 | tf_op jit(solution)/shard_map/ppermute | solution.py:19
  533.0 2.7 collective-permute-done.4
  535.7 1.8 collective-permute-done.5
  537.5 2.1 collective-permute-start.6
  539.6 2.2 collective-permute-start.7
  541.8 2.9 collective-permute-done.7
  547.9 2.9 copy-done.9
  550.8 8.1 %fusion.8 = f32[1,64,2048]{2,0,1:T(1,128)S(1)} fusion(bf16[27,64,2048]{2,1,0:T(8,128)(2,1)} %bitcast.1721, f32[16]{0:T(128)S(1)} %copy-done.10, bf16[27,16]{0,1:T(8,128)(2,1)S(1)} %copy-done, bf16[16]{0:T(256)(128)(2,1)S(1)} %copy-done.11), kind=kOutput, calls=%fused_computation.188 | convolution fusion | flops 123731968 | bytes 7603136 | tf_op jit(solution)/shard_map/n,nprc->prc/dot_general | solution.py:67
  558.9 1.2 fusion.248
  (305 shorter events, 29.1 us)
Async XLA Ops:
  7.2 543.6 %copy-start = (bf16[27,16]{0,1:T(8,128)(2,1)S(1)}, bf16[27,16]{0,1:T(8,128)(2,1)}, u32[]{:S(2)}) copy-start(bf16[27,16]{0,1:T(8,128)(2,1)} %param.13) | copy-start | bytes 2596
  7.2 432.2 %all-gather.3.cloned.1.call-start = ((), (), s32[]{:S(2)}) async-start(), calls=%async_computation | async-start | bytes 34078720 | tf_op jit(solution)/shard_map/all_gather | solution.py:50
  8.3 8.3 %collective-permute-start = (bf16[1,15,2048]{2,1,0:T(8,128)(2,1)S(1)}, bf16[1,15,2048]{2,1,0:T(8,128)(2,1)S(1)}, u32[]{:S(2)}, u32[]{:S(2)}) collective-permute-start(bf16[1,15,2048]{2,1,0:T(8,128)(2,1)S(1)} %get-tuple-element.351), channel_id=1, source_target_pairs={{0,1},{1,2},{2,3},{4,5},{5,6},{6,7},{8,9},{9,10},{10,11},{12,13},{... | collective-permute-start | bytes 184328 | tf_op jit(solution)/shard_map/ppermute | solution.py:16
  11.7 5.6 collective-permute-start.1
  17.4 0.7 copy-start.1
  39.0 9.3 %copy-start.2 = (bf16[94,2048]{1,0:T(8,128)(2,1)S(1)}, bf16[94,2048]{1,0:T(8,128)(2,1)}, u32[]{:S(2)}) copy-start(bf16[94,2048]{1,0:T(8,128)(2,1)} %copy-done.1) | copy-start | bytes 1155076
  92.0 6.7 %copy-start.8 = (bf16[1,31,31]{2,1,0:T(8,128)(2,1)S(1)}, bf16[1,31,31]{2,1,0:T(8,128)(2,1)}, u32[]{:S(2)}) copy-start(bf16[1,31,31]{2,1,0:T(8,128)(2,1)} %param.12) | copy-start | bytes 5770
  97.8 0.8 copy-start.5
  439.4 11.7 %copy-start.4 = (f32[64,2048]{1,0:T(8,128)S(1)}, f32[64,2048]{1,0:T(8,128)}, u32[]{:S(2)}) copy-start(f32[64,2048]{1,0:T(8,128)} %param.11) | copy-start | bytes 1572868
  451.2 8.8 %collective-permute-start.2 = (bf16[15,2048]{1,0:T(8,128)(2,1)S(1)}, bf16[15,2048]{1,0:T(8,128)(2,1)S(1)}, u32[]{:S(2)}, u32[]{:S(2)}) collective-permute-start(bf16[15,2048]{1,0:T(8,128)(2,1)S(1)} %get-tuple-element.349), channel_id=1, source_target_pairs={{0,1},{1,2},{2,3},{4,5},{5,6},{6,7},{8,9},{9,10},{10,11},{12,13},{... | collective-permute-start | bytes 184328 | tf_op jit(solution)/shard_map/ppermute | solution.py:16
  458.1 5.6 collective-permute-start.3
  515.7 5.3 copy-start.3
  515.7 5.3 copy-start.6
  515.7 5.3 copy-start.7
  522.0 13.7 %collective-permute-start.4 = (bf16[1,64,2048]{2,1,0:T(8,128)(2,1)S(1)}, bf16[1,64,2048]{2,1,0:T(8,128)(2,1)S(1)}, u32[]{:S(2)}, u32[]{:S(2)}) collective-permute-start(bf16[1,64,2048]{2,1,0:T(8,128)(2,1)S(1)} %get-tuple-element.5), channel_id=1, source_target_pairs={{0,4},{4,8},{8,12},{12,16},{16,20},{20,24},{24,28},{28,32},{32,36}... | collective-permute-start | bytes 786440 | tf_op jit(solution)/shard_map/ppermute | solution.py:16
  523.9 13.5 %collective-permute-start.5 = (bf16[1,64,2048]{2,1,0:T(8,128)(2,1)S(1)}, bf16[1,64,2048]{2,1,0:T(8,128)(2,1)S(1)}, u32[]{:S(2)}, u32[]{:S(2)}) collective-permute-start(bf16[1,64,2048]{2,1,0:T(8,128)(2,1)S(1)} %get-tuple-element.5), channel_id=1, source_target_pairs={{4,0},{8,4},{12,8},{16,12},{20,16},{24,20},{28,24},{32,28},{36,32}... | collective-permute-start | bytes 786440 | tf_op jit(solution)/shard_map/ppermute | solution.py:19
  537.5 4.3 collective-permute-start.6
  539.6 5.1 collective-permute-start.7
  547.3 3.5 copy-start.10
  547.4 3.4 copy-start.11
  547.9 2.9 copy-start.9
Sparse Core Ops, SparseCore 0:
  98.8 340.5 all-gather.2
